TPU v7x, 32 devices: a whole 2x2x4 slice. The times are simulated.
32 devices in a mesh: grp: 4 (over y, x), sub: 8 (over z, core).
Axes of the slice: x: 2, y: 2, z: 4, core: 2. Of those that a mesh axis runs over, the one named last changes fastest.
Arguments:
- solution: float32 [4, 8, 16, 512], P('grp', 'sub'), may hold values from -6 to 6
- residual: float32 [4, 8, 16, 512], P('grp', 'sub'), as said below
- direction: float32 [4, 8, 16, 512], P('grp', 'sub'), as said below
- inner_old: float32 [16], replicated, may hold values from 0.5 to 2
- interior: bfloat16 [4, 8, 16, 1536], P('grp', 'sub'), may hold values from -6 to 6
- weights: float32 [4, 8, 512], P('grp', 'sub'), as said below
- neighbours: int32 [4, 8, 4], P('grp', 'sub'), may hold values from -1 to 7, as said below
- coarse_rows: int32 [4, 8, 12], P('grp', 'sub'), may hold values from -1 to 119, as said below
- coarse_basis_matrix: float32 [4, 8, 12, 512], P('grp', 'sub'), may hold values from -0.5 to 0.5
- local_solver: bfloat16 [4, 8, 512, 512], P('grp', 'sub'), as said below
- schur_matrix: bfloat16 [4, 8, 512, 512], P('grp', 'sub'), as said below
- extension_values: bfloat16 [4, 8, 12, 2, 128, 128], P('grp', 'sub'), may hold values from -0.375 to 0.375
- extension_block_index: int32 [4, 8, 12, 2], P('grp', 'sub'), may hold values from 0 to 3
- coarse_inverse: float32 [120, 120], P('sub'), as said below
Outputs:
- solution_new: float32 [4, 8, 16, 512], P('grp', 'sub')
- residual_new: float32 [4, 8, 16, 512], P('grp', 'sub')
- direction_new: float32 [4, 8, 16, 512], P('grp', 'sub')
- interior_new: bfloat16 [4, 8, 16, 1536], P('grp', 'sub')
- inner_new: float32 [16], replicated
Inputs may be any that keep to these rules, and one draw needn't show every extreme that they name: Within a group the relation is symmetric: if neighbours[g, s, k] = t >= 0 then neighbours[g, t, k XOR 1] = s; the neighbours of one subdomain are distinct; -1 marks an absent block. `coarse_rows`: both subdomains of a shared face block list the same 3 rows for it, each coarse row is named by exactly two entries, and absent blocks hold -1. On a shared face the two sides' weights add up to 1; absent blocks hold 0. `residual`: equal on the two sides of every shared face, 0 on absent blocks. `direction`: equal on the two sides of every shared face, 0 on absent blocks. `local_solver`: Symmetric, with a positive diagonal larger than the sum of the magnitudes of its row's other entries. `schur_matrix`: Symmetric, with a positive diagonal larger than the sum of the magnitudes of its row's other entries. `coarse_inverse`: symmetric positive definite.
All inputs are finite; a program needn't handle non-finite values.
Results may differ from a plain program's by a relative error of at most 0.0019.
The roundings to bfloat16 on the way count: a program that leaves them out, or rounds other values in their place, can miss the bound.
Values sent between devices are 32-bit elements; how exact they have to be, the bound alone decides.
A program may use at most 64 MiB of HBM per device.

v0:
```python
import jax
import jax.numpy as jnp
from jax import lax
from jax.sharding import PartitionSpec as P

PRECISE = lax.Precision.HIGHEST


def contract(former, latter, former_dim, latter_dim):
    return lax.dot_general(
        former, latter, (((former_dim,), (latter_dim,)), ((), ())), precision=PRECISE
    )


def outgoing(blocks, neighbour, peer_count):
    active = (neighbour >= 0).astype(jnp.float32)
    clipped = jnp.maximum(neighbour, 0)
    outbound = jnp.transpose(blocks * active[None, :, None], (1, 0, 2))
    buffer = jnp.zeros((peer_count, blocks.shape[0], blocks.shape[2]), jnp.float32)
    return buffer.at[clipped].add(outbound)


def incoming(received, neighbour):
    active = (neighbour >= 0).astype(jnp.float32)
    picked = jnp.take(received, jnp.maximum(neighbour, 0), axis=0)
    return jnp.transpose(picked, (1, 0, 2)) * active[None, :, None]


def per_device(
    solution,
    residual,
    direction,
    inner_old,
    interior,
    weights,
    neighbours,
    coarse_rows,
    coarse_basis_matrix,
    local_solver,
    schur_matrix,
    extension_values,
    extension_block_index,
    coarse_inverse,
):
    peer_count = lax.axis_size("sub")
    rhs_count = residual.shape[2]
    local_faces = residual.shape[3]
    neighbour = neighbours[0, 0]
    slot_count = neighbour.shape[0]
    block_size = local_faces // slot_count
    active = jnp.repeat((neighbour >= 0).astype(jnp.float32), block_size)
    current = residual[0, 0]
    weight = weights[0, 0]
    basis_rows = coarse_basis_matrix[0, 0]
    primal = coarse_rows[0, 0]
    coarse_count = coarse_inverse.shape[1]
    face_total = coarse_count // (primal.shape[0] // slot_count) * block_size
    scaled = weight[None, :] * current
    local_solve = jnp.dot(
        scaled.astype(jnp.bfloat16), local_solver[0, 0], preferred_element_type=jnp.float32
    )
    coarse_part = contract(scaled, basis_rows, 1, 1)
    columns = lax.broadcasted_iota(jnp.int32, (primal.shape[0], coarse_count), 1)
    selector = (primal[:, None] == columns).astype(jnp.float32)
    partial_sum = jnp.dot(coarse_part, selector, precision=PRECISE)
    coarse_total = lax.psum(partial_sum, ("grp", "sub"))
    own_solution = contract(coarse_inverse, coarse_total, 1, 1)
    coarse_solution = lax.all_gather(own_solution, "sub", axis=0, tiled=True)
    coarse_local = jnp.dot(selector, coarse_solution, precision=PRECISE)
    correction = contract(coarse_local, basis_rows, 0, 0)
    weighted = weight[None, :] * (local_solve + correction)
    blocks_out = weighted.reshape(rhs_count, slot_count, block_size)
    received = lax.all_to_all(
        outgoing(blocks_out, neighbour, peer_count), "sub", split_axis=0, concat_axis=0, tiled=True
    )
    precond = weighted + incoming(received, neighbour).reshape(rhs_count, local_faces)
    inner_now = lax.psum(jnp.sum(current * precond, axis=1), ("grp", "sub")) / (2.0 * face_total)
    direction_new = precond + (inner_now / inner_old)[:, None] * direction[0, 0]
    direction_half = direction_new.astype(jnp.bfloat16)
    local_image = jnp.dot(direction_half, schur_matrix[0, 0], preferred_element_type=jnp.float32)
    image_blocks = local_image.reshape(rhs_count, slot_count, block_size)
    received_image = lax.all_to_all(
        outgoing(image_blocks, neighbour, peer_count),
        "sub",
        split_axis=0,
        concat_axis=0,
        tiled=True,
    )
    image_sum = active[None, :] * (
        local_image + incoming(received_image, neighbour).reshape(rhs_count, local_faces)
    )
    curve_term = 0.5 * jnp.sum(direction_new * image_sum, axis=1)
    curvature = lax.psum(curve_term, ("grp", "sub")) / face_total
    step_size = inner_now / curvature
    solution_new = solution[0, 0] + step_size[:, None] * direction_new
    residual_new = current - step_size[:, None] * image_sum
    direction_blocks = direction_half.reshape(rhs_count, slot_count, block_size)
    picked = jnp.take(direction_blocks, extension_block_index[0, 0], axis=1)
    extended = jnp.einsum(
        "rbjk,bjkl->rbl", picked, extension_values[0, 0], preferred_element_type=jnp.float32
    )
    extended = extended.reshape(rhs_count, -1)
    interior_new = (interior[0, 0].astype(jnp.float32) + step_size[:, None] * extended).astype(
        jnp.bfloat16
    )
    return (
        solution_new[None, None],
        residual_new[None, None],
        direction_new[None, None],
        interior_new[None, None],
        inner_now,
    )


def solution(mesh):
    in_specs = (
        P("grp", "sub", None, None),
        P("grp", "sub", None, None),
        P("grp", "sub", None, None),
        P(),
        P("grp", "sub", None, None),
        P("grp", "sub", None),
        P("grp", "sub", None),
        P("grp", "sub", None),
        P("grp", "sub", None, None),
        P("grp", "sub", None, None),
        P("grp", "sub", None, None),
        P("grp", "sub", None, None, None, None),
        P("grp", "sub", None, None),
        P("sub", None),
    )
    out_specs = (
        P("grp", "sub", None, None),
        P("grp", "sub", None, None),
        P("grp", "sub", None, None),
        P("grp", "sub", None, None),
        P(),
    )
    return jax.shard_map(
        per_device, mesh=mesh, in_specs=in_specs, out_specs=out_specs, check_vma=False
    )
```

profile of v0, /device:TPU:0, one launch (start us, length us, event | category | flops | bytes accessed | tf_op | source)
XLA Modules:
  0.0 169.0 jit_solution(9950449269539070436)
XLA Ops:
  0.7 0.7 fusion.35
  1.4 0.7 copy-done.8
  2.1 0.9 fusion.14
  3.0 0.7 copy-done.11
  3.9 42.0 %psum.21 = f32[16,120]{1,0:T(8,128)S(1)} all-reduce(f32[16,120]{1,0:T(8,128)S(1)} %fusion.32), channel_id=1, replica_groups=mesh['grp'=4,'sub'=8] {'grp','sub'}, use_global_device_ids=true, to_apply=%region_0.0 | all-reduce | flops 1920 | bytes 15360 | tf_op jit(solution)/shard_map/psum | solution.py:66
  46.1 1.2 fusion.4
  47.3 14.1 %all-gather = f32[8,15,16]{2,1,0:T(8,128)S(1)} all-gather(f32[1,15,16]{2,1,0:T(8,128)S(1)} %copy.35), channel_id=1, replica_groups=mesh['grp'=4,'sub'=8] {'sub'}, dimensions={0}, use_global_device_ids=true | all-gather | bytes 8640 | tf_op jit(solution)/shard_map/all_gather | solution.py:68
  61.6 0.3 fusion
  62.0 0.6 broadcast.107.clone
  62.6 2.0 %scatter_fusion = f32[8,16,128]{2,1,0:T(8,128)} fusion(f32[8,16,128]{2,1,0:T(8,128)} %broadcast.107.clone, s32[4]{0:T(128)S(1)} %maximum_bitcast_fusion, f32[4,16,128]{2,1,0:T(8,128)S(1)} %fusion.12), kind=kCustom, calls=%fused_computation.3 | custom fusion | flops 8192 | bytes 98320 | tf_op jit(solution)/shard_map/scatter-add | solution.py:20
  64.5 3.6 %all-to-all-start = ((f32[8,16,128]{2,1,0:T(8,128)}), f32[8,16,128]{2,1,0:T(8,128)S(1)}, u32[]{:S(2)}, u32[]{:S(2)}) async-start(f32[8,16,128]{2,1,0:T(8,128)} %scatter_fusion), calls=%async_computation | async-start | bytes 131072 | tf_op jit(solution)/shard_map/all_to_all | solution.py:73
  68.5 5.6 %all-to-all-done = f32[8,16,128]{2,1,0:T(8,128)S(1)} async-done(((f32[8,16,128]{2,1,0:T(8,128)}), f32[8,16,128]{2,1,0:T(8,128)S(1)}, u32[]{:S(2)}, u32[]{:S(2)}) %all-to-all-start) | async-done | bytes 65568 | tf_op jit(solution)/shard_map/all_to_all | solution.py:73
  74.1 0.5 gather_fusion.1
  74.9 39.3 %psum.22 = f32[16]{0:T(128)S(1)} all-reduce(f32[16]{0:T(128)S(1)} %fusion.20), channel_id=1, replica_groups=mesh['grp'=4,'sub'=8] {'grp','sub'}, use_global_device_ids=true, to_apply=%region_3.5 | all-reduce | flops 16 | bytes 128 | tf_op jit(solution)/shard_map/psum | solution.py:77
  114.6 0.6 broadcast.107
  115.2 2.0 %scatter_fusion.1 = f32[8,16,128]{2,1,0:T(8,128)} fusion(f32[8,16,128]{2,1,0:T(8,128)} %broadcast.107, s32[4]{0:T(128)S(1)} %maximum_bitcast_fusion, f32[4,16,128]{2,1,0:T(8,128)S(1)} %fusion.11), kind=kCustom, calls=%fused_computation.4 | custom fusion | flops 8192 | bytes 98320 | tf_op jit(solution)/shard_map/scatter-add | solution.py:20
  117.2 3.3 %all-to-all-start.1 = ((f32[8,16,128]{2,1,0:T(8,128)}), f32[8,16,128]{2,1,0:T(8,128)S(1)}, u32[]{:S(2)}, u32[]{:S(2)}) async-start(f32[8,16,128]{2,1,0:T(8,128)} %scatter_fusion.1), calls=%async_computation.1 | async-start | bytes 131072 | tf_op jit(solution)/shard_map/all_to_all | solution.py:82
  120.6 0.6 gather_fusion
  121.1 0.3 convolution_bitcast_fusion
  121.5 4.9 %all-to-all-done.1 = f32[8,16,128]{2,1,0:T(8,128)S(1)} async-done(((f32[8,16,128]{2,1,0:T(8,128)}), f32[8,16,128]{2,1,0:T(8,128)S(1)}, u32[]{:S(2)}, u32[]{:S(2)}) %all-to-all-start.1) | async-done | bytes 65568 | tf_op jit(solution)/shard_map/all_to_all | solution.py:82
  126.4 0.5 gather_fusion.2
  127.2 40.2 %psum.23 = f32[16]{0:T(128)S(1)} all-reduce(f32[16]{0:T(128)S(1)} %broadcast_multiply_fusion), channel_id=1, replica_groups=mesh['grp'=4,'sub'=8] {'grp','sub'}, use_global_device_ids=true, to_apply=%region_6.8 | all-reduce | flops 16 | bytes 128 | tf_op jit(solution)/shard_map/psum | solution.py:93
  167.5 0.7 fusion.21
  168.3 0.7 add_convert_fusion
  (55 shorter events, 2.0 us)
Async XLA Ops:
  0.6 120.5 %copy-start = (bf16[1,1,12,2,128,128]{5,4,3,2,1,0:T(8,128)(2,1)S(1)}, bf16[1,1,12,2,128,128]{5,4,3,2,1,0:T(8,128)(2,1)}, u32[]{:S(2)}) copy-start(bf16[1,1,12,2,128,128]{5,4,3,2,1,0:T(8,128)(2,1)} %param.27) | copy-start | bytes 2359300
  0.6 0.7 copy-start.14
  1.4 0.7 copy-start.8
  3.0 0.7 copy-start.11
  3.7 42.2 %copy-start.9 = (f32[15,120]{1,0:T(8,128)S(1)}, f32[15,120]{1,0:T(8,128)}, u32[]{:S(2)}) copy-start(f32[15,120]{1,0:T(8,128)} %param.29) | copy-start | bytes 21604
  3.9 42.3 %copy-start.1 = (f32[1,1,16,512]{3,2,1,0:T(8,128)S(1)}, f32[1,1,16,512]{3,2,1,0:T(8,128)}, u32[]{:S(2)}) copy-start(f32[1,1,16,512]{3,2,1,0:T(8,128)} %param.17) | copy-start | bytes 98308
  47.3 14.3 %copy-start.4 = (f32[1,1,12,512]{3,1,2,0:T(1,128)S(1)}, f32[1,1,12,512]{3,1,2,0:T(1,128)}, u32[]{:S(2)}) copy-start(f32[1,1,12,512]{3,1,2,0:T(1,128)} %param.24) | copy-start | bytes 73732
  61.4 52.9 %copy-start.3 = (bf16[1,1,512,512]{3,2,1,0:T(8,128)(2,1)S(1)}, bf16[1,1,512,512]{3,2,1,0:T(8,128)(2,1)}, u32[]{:S(2)}) copy-start(bf16[1,1,512,512]{3,2,1,0:T(8,128)(2,1)} %param.26) | copy-start | bytes 1572868
  64.5 3.6 %copy-start.10 = (s32[1,1,12,2]{2,3,1,0:T(2,128)S(1)}, s32[1,1,12,2]{2,3,1,0:T(2,128)}, u32[]{:S(2)}) copy-start(s32[1,1,12,2]{2,3,1,0:T(2,128)} %param.28) | copy-start | bytes 292
  64.5 9.5 %all-to-all-start = ((f32[8,16,128]{2,1,0:T(8,128)}), f32[8,16,128]{2,1,0:T(8,128)S(1)}, u32[]{:S(2)}, u32[]{:S(2)}) async-start(f32[8,16,128]{2,1,0:T(8,128)} %scatter_fusion), calls=%async_computation | async-start | bytes 131072 | tf_op jit(solution)/shard_map/all_to_all | solution.py:73
  74.6 39.6 %copy-start.7 = (f32[1,1,16,512]{3,2,1,0:T(8,128)S(1)}, f32[1,1,16,512]{3,2,1,0:T(8,128)}, u32[]{:S(2)}) copy-start(f32[1,1,16,512]{3,2,1,0:T(8,128)} %param.18) | copy-start | bytes 98308
  74.9 39.3 %copy-start.12 = (f32[16]{0:T(128)S(1)}, f32[16]{0:T(128)}, u32[]{:S(2)}) copy-start(f32[16]{0:T(128)} %param.19) | copy-start | bytes 196
  114.2 53.2 %copy-start.13 = (f32[16]{0:T(128)}, f32[16]{0:T(128)S(1)}, u32[]{:S(2)}) copy-start(f32[16]{0:T(128)S(1)} %get-tuple-element.9) | copy-start | bytes 196
  114.3 53.1 %copy-start.2 = (f32[16,512]{1,0:T(8,128)}, f32[16,512]{1,0:T(8,128)S(1)}, u32[]{:S(2)}) copy-start(f32[16,512]{1,0:T(8,128)S(1)} %get-tuple-element.7) | copy-start | bytes 98308
  117.2 9.2 %all-to-all-start.1 = ((f32[8,16,128]{2,1,0:T(8,128)}), f32[8,16,128]{2,1,0:T(8,128)S(1)}, u32[]{:S(2)}, u32[]{:S(2)}) async-start(f32[8,16,128]{2,1,0:T(8,128)} %scatter_fusion.1), calls=%async_computation.1 | async-start | bytes 131072 | tf_op jit(solution)/shard_map/all_to_all | solution.py:82
  127.2 40.3 %copy-start.6 = (f32[1,1,16,512]{3,2,1,0:T(8,128)S(1)}, f32[1,1,16,512]{3,2,1,0:T(8,128)}, u32[]{:S(2)}) copy-start(f32[1,1,16,512]{3,2,1,0:T(8,128)} %param.16) | copy-start | bytes 98308
  167.5 0.8 copy-start.5
where the time goes:
time: 170 us; the launch traced here: 169 us
  blocking collectives  136 us (80%)
  waiting for transfers between devices  10.5 us (6%)
  starting transfers between devices  6.94 us (4%)
  other arithmetic  6.72 us (4%)
  local copies, waits for them, and re-layouts  4.93 us (3%)
  matrix products  3.31 us (2%)
    psum x1, blocking collectives, per_device(): coarse_total = lax.psum(partial_sum, ('grp', 'sub'))  42 us
    psum x1, blocking collectives, per_device(): curvature = lax.psum(curve_term, ('grp', 'sub')) / face_total  40.2 us
    psum x1, blocking collectives, per_device(): lax.psum(jnp.sum(current * precond, axis=1), ('grp', 'sub'))  39.3 us
    all_gather x1, blocking collectives, per_device(): coarse_solution = lax.all_gather(own_solution, 'sub', axis=0, tiled=True)  14.1 us
    all_to_all x1, waiting for transfers between devices, per_device(): lax.all_to_all(outgoing(blocks_out, neighbour, peer_count), 'sub', split_...  5.6 us
    all_to_all x1, waiting for transfers between devices, per_device(): lax.all_to_all(outgoing(image_blocks, neighbour, peer_count), 'sub', spli...  4.94 us
    scatter-add x2, other arithmetic, outgoing(): return buffer.at[clipped].add(outbound)  3.91 us
    all_to_all x1, starting transfers between devices, per_device(): lax.all_to_all(outgoing(blocks_out, neighbour, peer_count), 'sub', split_...  3.59 us
  transfers between devices with their start and end apart: 2, of which 2 were waited for; matrix products, arithmetic and copies ran while one was open for 1% of the time, Pallas kernels for 0%

commit v1 on v0

--- a/solution.py
+++ b/solution.py
@@ -90,7 +90,7 @@
         local_image + incoming(received_image, neighbour).reshape(rhs_count, local_faces)
     )
     curve_term = 0.5 * jnp.sum(direction_new * image_sum, axis=1)
-    curvature = lax.psum(curve_term, ("grp", "sub")) / face_total
+    curvature = jax.lax.psum(jax.lax.psum(curve_term, "sub"), "grp") / face_total
     step_size = inner_now / curvature
     solution_new = solution[0, 0] + step_size[:, None] * direction_new
     residual_new = current - step_size[:, None] * image_sum

time: 170 us -> 154 us (0.906)
  blocking collectives: 136 us -> 120 us
    psum x1 -> x2, blocking collectives: 40.2 us -> 24.5 us  [the longest x1 13.8 us: per_device(): jax.lax.psum(curve_term, 'sub')]
where the time goes in v1:
time: 154 us; the launch traced here: 153 us
  blocking collectives  120 us (78%)
  waiting for transfers between devices  10.5 us (7%)
  starting transfers between devices  6.93 us (4%)
  other arithmetic  6.74 us (4%)
  local copies, waits for them, and re-layouts  4.94 us (3%)
  matrix products  3.31 us (2%)
    psum x1, blocking collectives, per_device(): coarse_total = lax.psum(partial_sum, ('grp', 'sub'))  42 us
    psum x1, blocking collectives, per_device(): lax.psum(jnp.sum(current * precond, axis=1), ('grp', 'sub'))  39.3 us
    all_gather x1, blocking collectives, per_device(): coarse_solution = lax.all_gather(own_solution, 'sub', axis=0, tiled=True)  14.1 us
    psum x1, blocking collectives, per_device(): jax.lax.psum(curve_term, 'sub')  13.8 us
    psum x1, blocking collectives, per_device(): jax.lax.psum(jax.lax.psum(curve_term, 'sub'), 'grp') / face_total  10.7 us
    all_to_all x1, waiting for transfers between devices, per_device(): lax.all_to_all(outgoing(blocks_out, neighbour, peer_count), 'sub', split_...  5.6 us
    all_to_all x1, waiting for transfers between devices, per_device(): lax.all_to_all(outgoing(image_blocks, neighbour, peer_count), 'sub', spli...  4.94 us
    scatter-add x2, other arithmetic, outgoing(): return buffer.at[clipped].add(outbound)  3.92 us
  transfers between devices with their start and end apart: 2, of which 2 were waited for; matrix products, arithmetic and copies ran while one was open for 1% of the time, Pallas kernels for 0%

profile of v1, /device:TPU:0, one launch (start us, length us, event | category | flops | bytes accessed | tf_op | source)
XLA Modules:
  0.0 153.2 jit_solution(13872363356411360387)
XLA Ops:
  0.7 0.7 fusion.35
  1.4 0.7 copy-done.8
  2.1 0.9 fusion.14
  3.0 0.7 copy-done.11
  3.9 42.0 %psum.28 = f32[16,120]{1,0:T(8,128)S(1)} all-reduce(f32[16,120]{1,0:T(8,128)S(1)} %fusion.32), channel_id=1, replica_groups=mesh['grp'=4,'sub'=8] {'grp','sub'}, use_global_device_ids=true, to_apply=%region_0.0 | all-reduce | flops 1920 | bytes 15360 | tf_op jit(solution)/shard_map/psum | solution.py:66
  46.1 1.2 fusion.4
  47.3 14.1 %all-gather = f32[8,15,16]{2,1,0:T(8,128)S(1)} all-gather(f32[1,15,16]{2,1,0:T(8,128)S(1)} %copy.35), channel_id=1, replica_groups=mesh['grp'=4,'sub'=8] {'sub'}, dimensions={0}, use_global_device_ids=true | all-gather | bytes 8640 | tf_op jit(solution)/shard_map/all_gather | solution.py:68
  62.0 0.6 broadcast.107.clone
  62.6 2.0 %scatter_fusion = f32[8,16,128]{2,1,0:T(8,128)} fusion(f32[8,16,128]{2,1,0:T(8,128)} %broadcast.107.clone, s32[4]{0:T(128)S(1)} %maximum_bitcast_fusion, f32[4,16,128]{2,1,0:T(8,128)S(1)} %fusion.12), kind=kCustom, calls=%fused_computation.3 | custom fusion | flops 8192 | bytes 98320 | tf_op jit(solution)/shard_map/scatter-add | solution.py:20
  64.6 3.6 %all-to-all-start = ((f32[8,16,128]{2,1,0:T(8,128)}), f32[8,16,128]{2,1,0:T(8,128)S(1)}, u32[]{:S(2)}, u32[]{:S(2)}) async-start(f32[8,16,128]{2,1,0:T(8,128)} %scatter_fusion), calls=%async_computation | async-start | bytes 131072 | tf_op jit(solution)/shard_map/all_to_all | solution.py:73
  68.5 5.6 %all-to-all-done = f32[8,16,128]{2,1,0:T(8,128)S(1)} async-done(((f32[8,16,128]{2,1,0:T(8,128)}), f32[8,16,128]{2,1,0:T(8,128)S(1)}, u32[]{:S(2)}, u32[]{:S(2)}) %all-to-all-start) | async-done | bytes 65568 | tf_op jit(solution)/shard_map/all_to_all | solution.py:73
  74.1 0.5 gather_fusion.1
  74.9 39.3 %psum.29 = f32[16]{0:T(128)S(1)} all-reduce(f32[16]{0:T(128)S(1)} %fusion.20), channel_id=1, replica_groups=mesh['grp'=4,'sub'=8] {'grp','sub'}, use_global_device_ids=true, to_apply=%region_3.5 | all-reduce | flops 16 | bytes 128 | tf_op jit(solution)/shard_map/psum | solution.py:77
  114.6 0.6 broadcast.107
  115.3 2.0 %scatter_fusion.1 = f32[8,16,128]{2,1,0:T(8,128)} fusion(f32[8,16,128]{2,1,0:T(8,128)} %broadcast.107, s32[4]{0:T(128)S(1)} %maximum_bitcast_fusion, f32[4,16,128]{2,1,0:T(8,128)S(1)} %fusion.11), kind=kCustom, calls=%fused_computation.4 | custom fusion | flops 8192 | bytes 98320 | tf_op jit(solution)/shard_map/scatter-add | solution.py:20
  117.2 3.3 %all-to-all-start.1 = ((f32[8,16,128]{2,1,0:T(8,128)}), f32[8,16,128]{2,1,0:T(8,128)S(1)}, u32[]{:S(2)}, u32[]{:S(2)}) async-start(f32[8,16,128]{2,1,0:T(8,128)} %scatter_fusion.1), calls=%async_computation.1 | async-start | bytes 131072 | tf_op jit(solution)/shard_map/all_to_all | solution.py:82
  120.6 0.6 gather_fusion
  121.2 0.3 convolution_bitcast_fusion
  121.5 4.9 %all-to-all-done.1 = f32[8,16,128]{2,1,0:T(8,128)S(1)} async-done(((f32[8,16,128]{2,1,0:T(8,128)}), f32[8,16,128]{2,1,0:T(8,128)S(1)}, u32[]{:S(2)}, u32[]{:S(2)}) %all-to-all-start.1) | async-done | bytes 65568 | tf_op jit(solution)/shard_map/all_to_all | solution.py:82
  126.4 0.5 gather_fusion.2
  127.2 13.8 %psum.30 = f32[16]{0:T(128)S(1)} all-reduce(f32[16]{0:T(128)S(1)} %broadcast_multiply_fusion), channel_id=1, replica_groups=mesh['grp'=4,'sub'=8] {'sub'}, use_global_device_ids=true, to_apply=%region_6.8 | all-reduce | flops 16 | bytes 128 | tf_op jit(solution)/shard_map/psum | solution.py:93
  141.0 10.7 %psum.31 = f32[16]{0:T(128)S(1)} all-reduce(f32[16]{0:T(128)S(1)} %psum.30), channel_id=1, replica_groups=mesh['grp'=4,'sub'=8] {'grp'}, use_global_device_ids=true, to_apply=%region_7.9 | all-reduce | flops 16 | bytes 128 | tf_op jit(solution)/shard_map/psum | solution.py:93
  151.7 0.7 fusion.21
  152.5 0.7 add_convert_fusion
  (56 shorter events, 2.2 us)
Async XLA Ops:
  0.6 120.5 %copy-start = (bf16[1,1,12,2,128,128]{5,4,3,2,1,0:T(8,128)(2,1)S(1)}, bf16[1,1,12,2,128,128]{5,4,3,2,1,0:T(8,128)(2,1)}, u32[]{:S(2)}) copy-start(bf16[1,1,12,2,128,128]{5,4,3,2,1,0:T(8,128)(2,1)} %param.27) | copy-start | bytes 2359300
  0.6 0.7 copy-start.14
  1.4 0.7 copy-start.8
  3.0 0.7 copy-start.11
  3.7 42.2 %copy-start.9 = (f32[15,120]{1,0:T(8,128)S(1)}, f32[15,120]{1,0:T(8,128)}, u32[]{:S(2)}) copy-start(f32[15,120]{1,0:T(8,128)} %param.29) | copy-start | bytes 21604
  3.9 42.3 %copy-start.1 = (f32[1,1,16,512]{3,2,1,0:T(8,128)S(1)}, f32[1,1,16,512]{3,2,1,0:T(8,128)}, u32[]{:S(2)}) copy-start(f32[1,1,16,512]{3,2,1,0:T(8,128)} %param.17) | copy-start | bytes 98308
  47.3 14.3 %copy-start.4 = (f32[1,1,12,512]{3,1,2,0:T(1,128)S(1)}, f32[1,1,12,512]{3,1,2,0:T(1,128)}, u32[]{:S(2)}) copy-start(f32[1,1,12,512]{3,1,2,0:T(1,128)} %param.24) | copy-start | bytes 73732
  61.4 52.9 %copy-start.3 = (bf16[1,1,512,512]{3,2,1,0:T(8,128)(2,1)S(1)}, bf16[1,1,512,512]{3,2,1,0:T(8,128)(2,1)}, u32[]{:S(2)}) copy-start(bf16[1,1,512,512]{3,2,1,0:T(8,128)(2,1)} %param.26) | copy-start | bytes 1572868
  64.6 3.6 %copy-start.10 = (s32[1,1,12,2]{2,3,1,0:T(2,128)S(1)}, s32[1,1,12,2]{2,3,1,0:T(2,128)}, u32[]{:S(2)}) copy-start(s32[1,1,12,2]{2,3,1,0:T(2,128)} %param.28) | copy-start | bytes 292
  64.6 9.5 %all-to-all-start = ((f32[8,16,128]{2,1,0:T(8,128)}), f32[8,16,128]{2,1,0:T(8,128)S(1)}, u32[]{:S(2)}, u32[]{:S(2)}) async-start(f32[8,16,128]{2,1,0:T(8,128)} %scatter_fusion), calls=%async_computation | async-start | bytes 131072 | tf_op jit(solution)/shard_map/all_to_all | solution.py:73
  74.6 39.6 %copy-start.7 = (f32[1,1,16,512]{3,2,1,0:T(8,128)S(1)}, f32[1,1,16,512]{3,2,1,0:T(8,128)}, u32[]{:S(2)}) copy-start(f32[1,1,16,512]{3,2,1,0:T(8,128)} %param.18) | copy-start | bytes 98308
  74.9 39.3 %copy-start.12 = (f32[16]{0:T(128)S(1)}, f32[16]{0:T(128)}, u32[]{:S(2)}) copy-start(f32[16]{0:T(128)} %param.19) | copy-start | bytes 196
  114.2 37.5 %copy-start.13 = (f32[16]{0:T(128)}, f32[16]{0:T(128)S(1)}, u32[]{:S(2)}) copy-start(f32[16]{0:T(128)S(1)} %get-tuple-element.9) | copy-start | bytes 196
  114.3 37.4 %copy-start.2 = (f32[16,512]{1,0:T(8,128)}, f32[16,512]{1,0:T(8,128)S(1)}, u32[]{:S(2)}) copy-start(f32[16,512]{1,0:T(8,128)S(1)} %get-tuple-element.7) | copy-start | bytes 98308
  117.2 9.2 %all-to-all-start.1 = ((f32[8,16,128]{2,1,0:T(8,128)}), f32[8,16,128]{2,1,0:T(8,128)S(1)}, u32[]{:S(2)}, u32[]{:S(2)}) async-start(f32[8,16,128]{2,1,0:T(8,128)} %scatter_fusion.1), calls=%async_computation.1 | async-start | bytes 131072 | tf_op jit(solution)/shard_map/all_to_all | solution.py:82
  141.0 10.7 %copy-start.6 = (f32[1,1,16,512]{3,2,1,0:T(8,128)S(1)}, f32[1,1,16,512]{3,2,1,0:T(8,128)}, u32[]{:S(2)}) copy-start(f32[1,1,16,512]{3,2,1,0:T(8,128)} %param.16) | copy-start | bytes 98308
  151.7 0.8 copy-start.5
